TPU v7x, 128 devices: a whole 4x4x4 slice. The times are simulated.
128 devices in a mesh: blk: 32 (over x, z, core), head: 4 (over y).
Axes of the slice: x: 4, y: 4, z: 4, core: 2. Of those that a mesh axis runs over, the one named last changes fastest.
Arguments:
- tokens_in: bfloat16 [2, 16384, 1024], P(None, ('blk', 'head')), may hold values from -6 to 6
- grad_out: bfloat16 [2, 16384, 1024], P(None, ('blk', 'head')), may hold values from -6 to 6
- flags: int32 [2, 32], P(None, 'blk'), may hold values from 0 to 1, as said below
- attn_gain: float32 [1024], replicated, may hold values from 0.1 to 1.9
- mlp_gain: float32 [1024], replicated, may hold values from 0.1 to 1.9
- w_qkv: bfloat16 [1024, 3, 1024], P(None, None, 'head'), may hold values from -0.1875 to 0.1875
- w_out: bfloat16 [1024, 1024], P('head'), may hold values from -0.75 to 0.75
- rel_bias: float32 [32, 8], P(None, 'head'), may hold values from -4 to 4
- state_query: bfloat16 [512, 1024], P(None, 'head'), may hold values from -5 to 5
- state_proj: bfloat16 [8, 128, 256], P('head'), may hold values from -0.5 to 0.5
- forget_bias: float32 [1024], P('head'), may hold values from -2 to 5
- forget_scale: float32 [1024], P('head'), may hold values from -6 to 6
- w_up: bfloat16 [1024, 4096], P(None, 'head'), may hold values from -0.1875 to 0.1875
- w_down: bfloat16 [4096, 1024], P('head'), may hold values from -0.09375 to 0.09375
Outputs:
- out_tokens: float32 [2, 16384, 1024], P(None, ('blk', 'head'))
- grad_tokens: float32 [2, 16384, 1024], P(None, ('blk', 'head'))
- block_states: float32 [2, 32, 512, 1024], P(None, 'blk', None, 'head')
- grad_attn_gain: float32 [1024], replicated
- grad_mlp_gain: float32 [1024], replicated
- grad_qkv: float32 [1024, 3, 1024], P(None, None, 'head')
- grad_out_proj: float32 [1024, 1024], P('head')
- grad_rel_bias: float32 [32, 8], P(None, 'head')
- grad_state_query: float32 [512, 1024], P(None, 'head')
- grad_state_proj: float32 [8, 128, 256], P('head')
- grad_forget_bias: float32 [1024], P('head')
- grad_forget_scale: float32 [1024], P('head')
- grad_up: float32 [1024, 4096], P(None, 'head')
- grad_down: float32 [4096, 1024], P('head')
Inputs may be any that keep to these rules, and one draw needn't show every extreme that they name: flags[m, 0] is 1 for every micro-batch; in one micro-batch drawn from the seed every other entry is 0.
All inputs are finite; a program needn't handle non-finite values.
Results may differ from a plain program's by a relative error of at most 0.025.
Values may be sent and summed in bfloat16 or wider, within the bound.
A program may use at most 256 MiB of HBM per device.

v0:
```python
import math
import types

import jax
import jax.numpy as jnp
from jax import lax
from jax.experimental import pallas as pl
from jax.experimental.pallas import tpu as pltpu
from jax.sharding import PartitionSpec as P

BUCKETS = 32
MAXDIST = 128
EPSILON = 1e-06
MASKED = -1e30
TILE = 128
MESH = pl.DeviceIdType.MESH
BF = jnp.bfloat16
F32 = jnp.float32
VMEM = pl.BlockSpec(memory_space=pltpu.VMEM)
SMEM = pl.BlockSpec(memory_space=pltpu.SMEM)
LIMIT = 60 * 2**20
ROOT = math.sqrt(2.0 / math.pi)
CUBIC = 0.044715


def bucket_starts():
    exact = BUCKETS // 2
    levels = [
        int(math.ceil(exact * (MAXDIST / exact) ** (t / (BUCKETS - exact))))
        for t in range(1, BUCKETS - exact)
    ]
    return list(range(exact + 1)) + levels


STARTS = bucket_starts()


def nn(a, b):
    return lax.dot_general(a, b, (((1,), (0,)), ((), ())), preferred_element_type=F32)


def nt(a, b):
    return lax.dot_general(a, b, (((1,), (1,)), ((), ())), preferred_element_type=F32)


def tn(a, b):
    return lax.dot_general(a, b, (((0,), (0,)), ((), ())), preferred_element_type=F32)


def inverse_rms(values):
    return lax.rsqrt(jnp.mean(values * values, axis=-1, keepdims=True) + EPSILON)


def tile_of(index, size=TILE):
    return pl.ds(pl.multiple_of(index * size, size), size)


def loop(count, step, after=None, action=None):
    def run(i, c):
        step(i)
        return c

    if after is not None:
        lax.fori_loop(0, after + 1, run, 0)
        action()
    lax.fori_loop(0 if after is None else after + 1, count, run, 0)


def remote(src, dst, send_sem, recv_sem, device):
    return pltpu.make_async_remote_copy(
        src_ref=src,
        dst_ref=dst,
        send_sem=send_sem,
        recv_sem=recv_sem,
        device_id=device,
        device_id_type=MESH,
    )


class Links:
    def __init__(self, send, recv):
        self.send, self.recv, self.used = send, recv, 0

    def go(self, src, dst, device):
        copy = remote(src, dst, self.send.at[self.used], self.recv.at[self.used], device)
        self.used += 1
        copy.start()
        return copy


class Ring:
    def __init__(self, links, me, device):
        self.links, self.me = links, me
        self.right = device(lax.rem(me + 1, 4))
        self.left = device(lax.rem(me + 3, 4))
        self.opposite = device(lax.rem(me + 2, 4))

    def go(self, src, dst, peer):
        return self.links.go(src, dst, peer)

    def greet(self):
        barrier = pltpu.get_barrier_semaphore()
        for peer in (self.right, self.left):
            pl.semaphore_signal(barrier, inc=1, device_id=peer, device_id_type=MESH)
        return 2

    def chunk(self, k):
        return lax.rem(self.me + k, 4)

    def row_chunk(self, k):
        return tile_of(self.chunk(k))


def head_ring(links):
    return Ring(links, lax.axis_index("head"), lambda i: {"head": i})


def by_rows(buf):
    half = buf.shape[1] // 2

    def piece(k, part=None, offset=0):
        return buf.at[k] if part is None else buf.at[k, part * half : (part + 1) * half]

    return piece


def by_columns(buf, base, rows, chunk):
    half = buf.shape[1] // 2
    starts = [pl.multiple_of(base + chunk(k) * rows, rows) for k in range(4)]

    def piece(k, part=None, offset=0):
        at = pl.ds(starts[(k + offset) % 4], rows)
        return buf.at[at] if part is None else buf.at[at, part * half : (part + 1) * half]

    return piece


class Gather:
    def __init__(self, ring, piece):
        self.ring, self.piece = ring, piece

    def start(self):
        r, p = self.ring, self.piece
        self.a0 = r.go(p(0, 0), p(3, 0, 1), r.right)
        self.b0 = r.go(p(0, 1), p(1, 1, 3), r.left)
        self.a1 = r.go(p(0, 1), p(3, 1, 1), r.right)
        self.b1 = r.go(p(0, 0), p(1, 0, 3), r.left)

    def relay(self):
        r, p = self.ring, self.piece
        self.a0.wait_recv()
        self.a2 = r.go(p(3, 0), p(2, 0, 1), r.right)
        self.b0.wait_recv()
        self.b2 = r.go(p(1, 1), p(2, 1, 3), r.left)

    def finish(self):
        for copy in (self.a1, self.b1, self.a2, self.b2):
            copy.wait_recv()

    def close(self):
        for copy in (self.a0, self.b0, self.a1, self.b1, self.a2, self.b2):
            copy.wait_send()


class Reduce:
    def __init__(self, ring, terms, mid, into):
        self.ring, self.terms, self.mid, self.into = ring, terms, mid, into
        if mid.shape[1] == into.shape[1]:
            half = into.shape[2] // 2
            self.place = lambda i, part: into.at[i, :, part * half : (part + 1) * half]
        else:
            half = into.shape[1] // 2
            self.place = lambda i, part: into.at[i, part * half : (part + 1) * half]

    def start(self):
        r, t = self.ring, self.terms
        self.a0 = r.go(t(2, 0), self.mid.at[0], r.right)
        self.b0 = r.go(t(2, 1), self.mid.at[1], r.left)
        self.a1 = r.go(t(1, 1), self.place(0, 1), r.right)
        self.b1 = r.go(t(3, 0), self.place(1, 0), r.left)

    def relay(self):
        r, t, mid = self.ring, self.terms, self.mid
        self.a0.wait_recv()
        mid[2] = (mid[0].astype(F32) + t(1, 0)[...].astype(F32)).astype(BF)
        self.a2 = r.go(mid.at[2], self.place(0, 0), r.right)
        self.b0.wait_recv()
        mid[3] = (mid[1].astype(F32) + t(3, 1)[...].astype(F32)).astype(BF)
        self.b2 = r.go(mid.at[3], self.place(1, 1), r.left)

    def finish(self):
        for copy in (self.a1, self.b1, self.a2, self.b2):
            copy.wait_recv()
        return (
            self.terms(0)[...].astype(F32)
            + self.into[0].astype(F32)
            + self.into[1].astype(F32)
        )

    def close(self):
        for copy in (self.a0, self.b0, self.a1, self.b1, self.a2, self.b2):
            copy.wait_send()


def block_device(x, z, c):
    return {"blk": (x * 4 + z) * 2 + c}


def block_place():
    place = lax.axis_index("blk")
    return place % 2, (place // 2) % 4, place // 8


class Plane:
    def __init__(self, links):
        c, z, x = block_place()
        self.links = links
        self.peer = block_device(x, z, 1 - c)
        rx = Ring(links, x, lambda i: block_device(i, z, c))
        rz = Ring(links, z, lambda i: block_device(x, i, c))
        self.rings = [rx, rz]
        self.first, self.second = (rx, rz), (rz, rx)
        self.base = c * 512
        self.own = pl.ds(pl.multiple_of(c * 512, 512), 512)
        self.away = pl.ds(pl.multiple_of((1 - c) * 512, 512), 512)
        self.top = [c * 512 + x * 64, c * 512 + 256 + z * 64]
        self.last = [
            pl.ds(pl.multiple_of(self.top[0] + z * 16, 16), 16),
            pl.ds(pl.multiple_of(self.top[1] + x * 16, 16), 16),
        ]

    def greet(self):
        barrier = pltpu.get_barrier_semaphore()
        pl.semaphore_signal(barrier, inc=1, device_id=self.peer, device_id_type=MESH)
        return 1 + sum(ring.greet() for ring in self.rings)


class Steps:
    def advance(self, steps=1):
        for _ in range(steps):
            if self.steps:
                self.steps.pop(0)()


class CoreSum:
    def __init__(self, plane, parts, half):
        self.plane, self.parts, self.half = plane, parts, half

    def start(self):
        plane = self.plane
        self.swap = plane.links.go(self.parts.at[plane.away], self.half, plane.peer)

    def finish(self):
        self.swap.wait_recv()

        def add(t):
            rows = tile_of(t, 64)
            own = pl.ds(pl.multiple_of(self.plane.base + t * 64, 64), 64)
            self.half[rows] = (
                self.parts[own].astype(F32) + self.half[rows].astype(F32)
            ).astype(BF)

        loop(8, add)

    def close(self):
        self.swap.wait_send()


class PlaneReduce(Steps):
    def __init__(self, plane, half, total, mid, into, quarter, small_into):
        self.plane, self.half, self.total, self.quarter = plane, half, total, quarter
        first, second = plane.first, plane.second
        self.reduce1 = [
            Reduce(first[i], by_columns(half, i * 256, 64, first[i].chunk), mid.at[i], into.at[i])
            for i in range(2)
        ]
        self.reduce2 = [
            ReduceDirect(
                second[i], by_columns(quarter.at[i], 0, 16, second[i].chunk), small_into.at[i]
            )
            for i in range(2)
        ]
        self.steps = [
            lambda: [r.start() for r in self.reduce1],
            lambda: [r.relay() for r in self.reduce1],
            self.start2,
            self.finish,
        ]

    def start2(self):
        for i, r in enumerate(self.reduce1):
            self.quarter[i] = r.finish().astype(BF)
            self.reduce2[i].start()

    def finish(self):
        for i, r in enumerate(self.reduce2):
            self.total[self.plane.last[i]] = r.finish().astype(BF)

    def close(self):
        for r in self.reduce1 + self.reduce2:
            r.close()


class PlaneGather(Steps):
    def __init__(self, plane, total):
        self.plane, self.total = plane, total
        first, second = plane.first, plane.second
        self.gather1 = [
            GatherDirect(second[i], by_columns(total, plane.top[i], 16, second[i].chunk))
            for i in range(2)
        ]
        self.gather2 = [
            Gather(first[i], by_columns(total, plane.base + i * 256, 64, first[i].chunk))
            for i in range(2)
        ]
        self.steps = [
            lambda: [g.start() for g in self.gather1],
            self.start2,
            lambda: [g.relay() for g in self.gather2],
            self.cores,
            lambda: self.swap.wait_recv(),
        ]

    def start2(self):
        for i, g in enumerate(self.gather1):
            g.finish()
            self.gather2[i].start()

    def cores(self):
        for g in self.gather2:
            g.finish()
        rows = self.total.at[self.plane.own]
        self.swap = self.plane.links.go(rows, rows, self.plane.peer)

    def close(self):
        self.swap.wait_send()
        for g in self.gather1 + self.gather2:
            g.close()


def reduce_scratch(name, width):
    return {
        name + "mid": ((2, 4, 64, width // 2), BF),
        name + "into": ((2, 2, 64, width), BF),
        name + "quarter": ((2, 64, width), BF),
        name + "small": ((2, 3, 16, width), BF),
    }


class GatherDirect:
    def __init__(self, ring, piece):
        self.ring, self.piece = ring, piece

    def start(self):
        r, p = self.ring, self.piece
        self.copies = [
            r.go(p(0), p(4 - k, None, k), peer)
            for k, peer in ((1, r.right), (3, r.left), (2, r.opposite))
        ]

    def finish(self):
        for copy in self.copies:
            copy.wait_recv()

    def close(self):
        for copy in self.copies:
            copy.wait_send()


class ReduceDirect:
    def __init__(self, ring, terms, into):
        self.ring, self.terms, self.into = ring, terms, into

    def start(self):
        r, t = self.ring, self.terms
        self.copies = [
            r.go(t(k), self.into.at[k - 1], peer)
            for k, peer in ((1, r.right), (3, r.left), (2, r.opposite))
        ]

    def finish(self):
        for copy in self.copies:
            copy.wait_recv()
        total = self.terms(0)[...].astype(F32)
        for k in range(3):
            total = total + self.into[k].astype(F32)
        return total

    def close(self):
        for copy in self.copies:
            copy.wait_send()


class Exchange:
    def __init__(self, source, target, send, recv, local):
        self.count = lax.axis_size("blk")
        self.place = lax.axis_index("blk")
        self.size = source.shape[0] // self.count
        self.source, self.target = source, target
        self.send, self.recv, self.local = send, recv, local

    def part(self, j):
        peer = lax.rem(self.place + j, self.count)
        return remote(
            self.source.at[tile_of(peer, self.size)],
            self.target.at[tile_of(self.place, self.size)],
            self.send.at[j],
            self.recv.at[j],
            {"blk": peer},
        )

    def own(self):
        rows = tile_of(self.place, self.size)
        return pltpu.make_async_copy(self.source.at[rows], self.target.at[rows], self.local)

    def start(self):
        loop(self.count - 1, lambda j: self.part(j + 1).start())
        self.own().start()

    def finish(self):
        self.own().wait()
        loop(self.count - 1, lambda j: self.part(j + 1).wait_recv())

    def close(self):
        loop(self.count - 1, lambda j: self.part(j + 1).wait_send())


def greet_blocks():
    barrier = pltpu.get_barrier_semaphore()
    count, place = lax.axis_size("blk"), lax.axis_index("blk")

    def greet(j):
        pl.semaphore_signal(
            barrier, inc=1, device_id={"blk": lax.rem(place + j + 1, count)}, device_id_type=MESH
        )

    loop(count - 1, greet)
    return count - 1


def closed_row(flag, qi):
    column = lax.broadcasted_iota(jnp.int32, (1, 5 * TILE), 1) + qi * TILE
    return jnp.where(column < 512, MASKED * flag.astype(F32), 0.0)


def head(h, size=TILE, base=0):
    return slice(base + h * size, base + (h + 1) * size)


def window_of(qi):
    return pl.ds(pl.multiple_of(qi * TILE, TILE), 5 * TILE)


def split_rows(target, m, cols, part):
    for k in range(4):
        target[m, k, :, cols] = part[k * TILE : (k + 1) * TILE]


def write_table(table, rel):
    row = lax.broadcasted_iota(jnp.int32, (TILE, TILE), 0)
    col = lax.broadcasted_iota(jnp.int32, (TILE, TILE), 1)

    def per_head(h):
        far = jnp.full((TILE, TILE), rel[h, BUCKETS - 1], F32)
        table[h, :, 0:128] = jnp.where(row < col, far, MASKED)
        table[h, :, 128:256] = far
        table[h, :, 256:384] = far
        for shift, at in ((TILE, 384), (0, 512)):
            distance = row - col + shift
            total = jnp.full((TILE, TILE), rel[h, 0], F32)
            for t in range(1, BUCKETS):
                total = jnp.where(distance >= STARTS[t], rel[h, t], total)
            table[h, :, at : at + TILE] = jnp.where(distance >= 0, total, MASKED)

    loop(2, per_head)


def forward_kernel(r):
    scale = TILE**-0.5
    links = Links(r.send, r.recv)
    ring = head_ring(links)
    plane = Plane(links)
    place, count = lax.axis_index("blk"), lax.axis_size("blk")
    both = range(2)

    def norm_rows(m):
        rows = r.x[m].astype(F32)
        r.whole.ref[m, 0] = (rows * inverse_rms(rows) * r.attn_gain[...]).astype(BF)

    norm_rows(0)
    for m in both:
        keep = 1.0 - r.flags[0, m].astype(F32)
        r.own_keep[m : m + 1] = jnp.full((1, 256), keep, F32)
    r.own_keep[2:8] = jnp.zeros((6, 256), F32)
    pl.semaphore_wait(pltpu.get_barrier_semaphore(), ring.greet() + greet_blocks())
    whole, qkv, kv_all = r.whole.ref, r.qkv.ref, r.kv_all.ref
    prior, across, keeps = r.prior.ref, r.across.ref, r.keeps.ref
    update, stats, state_kv = r.update.ref, r.stats.ref, r.state_kv.ref
    table, att_rel, middle, branch = r.table.ref, r.att_rel.ref, r.middle.ref, r.branch.ref
    gather_x = [Gather(ring, by_rows(whole.at[m])) for m in both]
    gather_g = [Gather(ring, by_rows(r.whole_grad.at[m])) for m in both]
    gather_x[0].start()
    norm_rows(1)

    def tell(j):
        peer = {"blk": lax.rem(place + j, count)}
        return remote(r.own_keep, keeps.at[place], r.s3.at[j], r.r3.at[j], peer)

    loop(count - 1, lambda j: tell(j + 1).start())
    keeps[place] = r.own_keep[...]
    write_table(table, r.rel)
    r.table.put()
    after = {"blk": lax.rem(place + 1, count)}
    shifts = [
        remote(qkv.at[m, :, 256:768], kv_all.at[m, 0:512], r.s0.at[m], r.r0.at[m], after)
        for m in both
    ]
    there = [
        Exchange(r.unit_low.at[m], across.at[m], r.s1.at[m], r.r1.at[m], r.local.at[m])
        for m in both
    ]
    back = [
        Exchange(r.held.at[m], prior.at[m], r.s2.at[m], r.r2.at[m], r.local.at[2 + m])
        for m in both
    ]

    def project(m):
        def columns(n):
            cols = tile_of(n, 256)
            part = nn(whole[m].reshape(512, 1024), r.w.ref[n]).astype(BF)
            for k in range(4):
                qkv[m, ring.row_chunk(k), cols] = part[k * TILE : (k + 1) * TILE]

        loop(3, columns)
        shifts[m].start()
        kv_all[m, 512:1024] = qkv[m, :, 256:768]

    def update_tile(m):
        def step(t):
            rows = tile_of(t)
            for h in range(2):
                scores = nt(r.state_query.ref[rows, head(h)], qkv[m, :, head(h, base=256)]) * scale
                top = jnp.max(scores, axis=-1, keepdims=True)
                raised = jnp.exp(scores - top)
                total = jnp.sum(raised, axis=-1, keepdims=True)
                stats[m, rows, h : h + 1] = top + jnp.log(total)
                u = nn(raised.astype(BF), qkv[m, :, head(h, base=512)]) / total
                update[m, rows, head(h)] = u
                r.unit_low[m, rows, head(h)] = (u * inverse_rms(u)).astype(BF)

        return step

    def scan(m):
        def step(b, state):
            rows = tile_of(b, 16)
            u = across[m, rows].astype(F32)
            forget = jax.nn.sigmoid(r.bias[...] + r.slope[...] * u)
            before = keeps[b, m : m + 1] * state
            r.held[m, rows] = before.astype(BF)
            return forget * before + (1.0 - forget) * u

        lax.fori_loop(0, count, step, jnp.zeros((16, 256), F32))

    def state(m):
        def step(t):
            rows = tile_of(t)
            before = prior[m, rows]
            for h in range(2):
                state_kv[m, rows, head(h, 256)] = nn(before[:, head(h)], r.state_proj.ref[h]).astype(BF)
                u = update[m, rows, head(h)]
                u = u * inverse_rms(u)
                forget = jax.nn.sigmoid(r.bias[:, head(h)] + r.slope[:, head(h)] * u)
                r.state_after.ref[m, rows, head(h)] = (
                    forget * before[:, head(h)].astype(F32) + (1.0 - forget) * u
                )

        return step

    def attend(m):
        def step(qi):
            rows, window = tile_of(qi), window_of(qi)
            shut = closed_row(r.flags[0, m], qi)
            for h in range(2):
                q = qkv[m, rows, head(h)]
                token = nt(q, kv_all[m, window, head(h)]) * scale + (table[h] + shut)
                from_state = nt(q, state_kv[m, :, h * 256 : h * 256 + TILE]) * scale
                top = jnp.maximum(
                    jnp.max(token, axis=-1, keepdims=True),
                    jnp.max(from_state, axis=-1, keepdims=True),
                )
                token = jnp.exp(token - top)
                from_state = jnp.exp(from_state - top)
                total = jnp.sum(token, axis=-1, keepdims=True) + jnp.sum(
                    from_state, axis=-1, keepdims=True
                )
                stats[m, rows, 2 + h : 3 + h] = top + jnp.log(total)
                out = nn(token.astype(BF), kv_all[m, window, head(h, base=256)]) + nn(
                    from_state.astype(BF), state_kv[m, :, h * 256 + TILE : (h + 1) * 256]
                )
                att_rel[m, lax.rem(qi + 4 - ring.me, 4), :, head(h)] = (out / total).astype(BF)

        return step

    first = [
        Reduce(ring, by_rows(r.terms.at[m]), r.mids.at[m], r.intos.at[m]) for m in both
    ]
    second = [Gather(ring, by_rows(r.whole_mlp.at[m])) for m in both]
    third = [
        Reduce(ring, by_rows(r.terms.at[m]), r.mids.at[2 + m], r.intos.at[2 + m]) for m in both
    ]
    fourth = Gather(ring, by_rows(r.gm0))

    def out_terms(m):
        def columns(n):
            cols = tile_of(n, 256)
            part = nn(att_rel[m].reshape(512, 256), r.w_out.ref[:, cols]).astype(BF)
            split_rows(r.terms, m, cols, part)

        loop(4, columns)

    def normalise(m):
        rows = r.x[m].astype(F32) + first[m].finish()
        middle[m] = rows
        r.whole_mlp[m, 0] = (rows * inverse_rms(rows) * r.mlp_gain[...]).astype(BF)

    def hidden(m):
        def columns(n):
            cols = tile_of(n, 256)
            value = nn(r.whole_mlp[m].reshape(512, 1024), r.w_up.ref[:, cols])
            grad_active = nt(r.whole_grad[m].reshape(512, 1024), r.w_down.ref[cols])
            square = value * value
            bent = jnp.tanh(ROOT * value * (1.0 + CUBIC * square))
            r.active[m, :, cols] = (0.5 * value * (1.0 + bent)).astype(BF)
            rise = 0.5 * (1.0 + bent) + 0.5 * value * (1.0 - bent * bent) * ROOT * (
                1.0 + 3.0 * CUBIC * square
            )
            r.grad_hidden[m, :, cols] = (grad_active * rise).astype(BF)

        return columns

    def grad_terms(m):
        def columns(n):
            cols = tile_of(n, 256)
            part = nt(r.grad_hidden[m], r.w_up.ref[cols]).astype(BF)
            split_rows(r.terms, m, cols, part)

        loop(4, columns)

    def branch_terms(m):
        def columns(n):
            cols = tile_of(n, 256)
            part = nn(r.active[m], r.w_down.ref[:, cols]).astype(BF)
            split_rows(branch, m, cols, part)

        loop(4, columns)

    def grad_rows(m):
        grad_normed = third[m].finish()
        rows = middle[m]
        inverse = inverse_rms(rows)
        unit = rows * inverse
        part = jnp.sum(grad_normed * unit, axis=0, keepdims=True)
        r.g_gain[...] = part if m == 0 else r.g_gain[...] + part
        scaled = grad_normed * r.mlp_gain[...]
        inner = jnp.mean(scaled * unit, axis=-1, keepdims=True)
        total = r.g.ref[m].astype(F32) + inverse * (scaled - unit * inner)
        r.grad_middle[m] = total
        if m == 0:
            r.gm0[0] = total.astype(BF)

    def up_rows(n):
        rows = tile_of(n, 256)
        total = tn(r.whole_mlp[0, :, :, rows].reshape(512, 256), r.grad_hidden[0])
        total = total + tn(r.whole_mlp[1, :, :, rows].reshape(512, 256), r.grad_hidden[1])
        r.parts[rows, 0:1024] = total.astype(BF)

    def down_rows(n):
        rows = tile_of(n, 256)
        total = tn(r.active[0, :, rows], r.whole_grad[0].reshape(512, 1024))
        total = total + tn(r.active[1, :, rows], r.whole_grad[1].reshape(512, 1024))
        r.parts[rows, 1024:2048] = total.astype(BF)

    cores = CoreSum(plane, r.parts, r.half)

    gather_x[0].relay()
    gather_x[1].start()
    r.w.get()
    gather_x[0].finish()
    project(0)
    gather_x[1].relay()
    r.state_query.get()
    loop(4, update_tile(0))
    there[0].start()
    gather_x[1].finish()
    r.g.get()
    for m in both:
        r.whole_grad[m, 0] = r.g.ref[m]
    gather_g[0].start()
    project(1)
    r.whole.put()
    r.qkv.put()
    loop(4, update_tile(1))
    there[1].start()
    r.update.put()
    gather_g[0].relay()
    gather_g[1].start()
    loop(count - 1, lambda j: tell(j + 1).wait_recv())
    there[0].finish()
    scan(0)
    back[0].start()
    there[1].finish()
    scan(1)
    back[1].start()
    gather_g[1].relay()
    r.across.put()
    r.keeps.put()
    shifts[0].wait_recv()
    shifts[1].wait_recv()
    r.kv_all.put()
    r.state_proj.get()
    back[0].finish()
    loop(4, state(0))
    loop(4, attend(0))
    r.w_out.get()
    out_terms(0)
    first[0].start()
    back[1].finish()
    r.prior.put()
    loop(4, state(1))
    r.state_kv.put()
    r.state_after.put()
    loop(4, attend(1), 0, first[0].relay)
    r.stats.put()
    out_terms(1)
    r.att_rel.put()
    first[1].start()
    normalise(0)
    second[0].start()
    first[1].relay()
    second[0].relay()
    r.w_up.get()
    r.w_down.get()
    gather_g[0].finish()
    gather_g[1].finish()
    normalise(1)
    second[1].start()
    r.middle.put()
    second[0].finish()
    loop(4, hidden(0), 1, second[1].relay)
    first[0].close()
    grad_terms(0)
    third[0].start()
    second[1].finish()
    loop(4, hidden(1), 1, third[0].relay)
    first[1].close()
    grad_terms(1)
    third[1].start()
    loop(4, up_rows)
    grad_rows(0)
    fourth.start()
    third[1].relay()
    loop(4, down_rows)
    cores.start()
    fourth.relay()
    branch_terms(0)
    branch_terms(1)
    r.branch.put()
    cores.finish()
    grad_rows(1)
    fourth.finish()
    cores.close()
    fourth.close()
    for m in both:
        for step in (gather_x, gather_g, second, third):
            step[m].close()
        shifts[m].wait_send()
        there[m].close()
        back[m].close()
    loop(count - 1, lambda j: tell(j + 1).wait_send())


def backward_kernel(r):
    scale = TILE**-0.5
    links = Links(r.send, r.recv)
    ring = head_ring(links)
    plane = Plane(links)
    place, count = lax.axis_index("blk"), lax.axis_size("blk")
    both = range(2)
    gm = [r.gm0, r.gm1]
    r.gm1[0] = r.grad_middle[1].astype(BF)
    core = place % 2
    others = [
        {"head": ring.chunk(k), "blk": place - core + c} for k in range(1, 4) for c in range(2)
    ]
    barrier = pltpu.get_barrier_semaphore()
    for device in others:
        pl.semaphore_signal(barrier, inc=1, device_id=device, device_id_type=MESH)
    pl.semaphore_wait(barrier, len(others) + greet_blocks())
    fourth = Gather(ring, by_rows(r.gm1))
    fourth.start()
    mlp_sum = PlaneReduce(
        plane, r.half, r.total_mlp, r.mlp_mid, r.mlp_into, r.mlp_quarter, r.mlp_small
    )
    mlp_all = PlaneGather(plane, r.total_mlp)
    mlp_sum.advance()
    qkv, kv_all, state_kv, stats = r.qkv.ref, r.kv_all.ref, r.state_kv.ref, r.stats.ref
    r.branch.get()
    branch = r.branch.ref
    outs = [Reduce(ring, by_rows(branch.at[m]), r.mids.at[m], r.intos.at[m]) for m in both]
    ends = [
        Reduce(ring, by_rows(branch.at[m]), r.mids.at[2 + m], r.intos.at[2 + m]) for m in both
    ]
    before = {"blk": lax.rem(place + count - 1, count)}
    shifts = [
        remote(r.early.at[m], r.later.at[m], r.s0.at[m], r.r0.at[m], before) for m in both
    ]
    there = [
        Exchange(r.grad_prior.at[m], r.moved.at[m], r.s1.at[m], r.r1.at[m], r.local.at[m])
        for m in both
    ]
    back = [
        Exchange(r.held.at[m], r.grad_after.at[m], r.s2.at[m], r.r2.at[m], r.local.at[2 + m])
        for m in both
    ]
    for ref in (r.near, r.sums, r.g_query, r.g_bias, r.g_scale, r.grad_kv, r.grad_state):
        ref[...] = jnp.zeros(ref.shape, F32)

    def own_chunk(qi):
        return lax.rem(qi + 4 - ring.me, 4)

    def attention_rows(m):
        part = nt(gm[m][...].reshape(512, 1024), r.w_out[...]).astype(BF)
        for k in range(4):
            r.grad_att[m, ring.row_chunk(k)] = part[k * TILE : (k + 1) * TILE]

    def attend(m):
        def step(qi):
            rows, window = tile_of(qi), window_of(qi)
            shut = closed_row(r.flags[0, m], qi)
            for h in range(2):
                k_cols, v_cols = head(h), head(h, base=256)
                sk_cols = slice(h * 256, h * 256 + TILE)
                sv_cols = slice(h * 256 + TILE, (h + 1) * 256)
                q = qkv[m, rows, head(h)]
                d = r.grad_att[m, rows, head(h)]
                level = stats[m, rows, 2 + h : 3 + h]
                token = jnp.exp(
                    nt(q, kv_all[m, window, k_cols]) * scale + (r.table.ref[h] + shut) - level
                )
                from_state = jnp.exp(nt(q, state_kv[m, :, sk_cols]) * scale - level)
                grad_token = nt(d, kv_all[m, window, v_cols])
                grad_from = nt(d, state_kv[m, :, sv_cols])
                delta = jnp.sum(token * grad_token, axis=-1, keepdims=True) + jnp.sum(
                    from_state * grad_from, axis=-1, keepdims=True
                )
                grad_token = token * (grad_token - delta)
                grad_from = from_state * (grad_from - delta)
                r.near[h, :, 0:128] += (
                    grad_token[:, 0:128] + grad_token[:, 128:256] + grad_token[:, 256:384]
                )
                r.near[h, :, 128:384] += grad_token[:, 384:640]
                token_low = grad_token.astype(BF)
                from_low = grad_from.astype(BF)
                grad_q = scale * (
                    nn(token_low, kv_all[m, window, k_cols]) + nn(from_low, state_kv[m, :, sk_cols])
                )
                r.dqkv[m, own_chunk(qi), :, head(h)] = grad_q.astype(BF)
                r.grad_kv[m, window, k_cols] += tn(token_low, q)
                r.grad_kv[m, window, v_cols] += tn(token.astype(BF), d)
                r.grad_state[m, :, sk_cols] += tn(from_low, q)
                r.grad_state[m, :, sv_cols] += tn(from_state.astype(BF), d)

        return step

    def pass_on(m):
        r.early[m, :, 0:256] = (scale * r.grad_kv[m, 0:512, 0:256]).astype(BF)
        r.early[m, :, 256:512] = r.grad_kv[m, 0:512, 256:512].astype(BF)
        for h in range(2):
            low = jnp.concatenate(
                [
                    (scale * r.grad_state[m, :, h * 256 : h * 256 + TILE]).astype(BF),
                    r.grad_state[m, :, h * 256 + TILE : (h + 1) * 256].astype(BF),
                ],
                1,
            )
            r.grad_prior[m, :, head(h)] = nt(low, r.state_proj.ref[h]).astype(BF)
            part = tn(r.prior.ref[m, :, head(h)], low)
            r.g_proj[h] = part if m == 0 else r.g_proj[h] + part
        there[m].start()
        shifts[m].start()

    def scan(m):
        def step(t, grad):
            b = count - 1 - t
            rows = tile_of(b, 16)
            r.held[m, rows] = grad.astype(BF)
            u = r.across.ref[m, rows].astype(F32)
            forget = jax.nn.sigmoid(r.bias[...] + r.slope[...] * u)
            moved = r.moved[m, rows].astype(F32)
            return r.keeps.ref[b, m : m + 1] * (moved + forget * grad)

        lax.fori_loop(0, count, step, jnp.zeros((16, 256), F32))

    def bucket_sums():
        row = lax.broadcasted_iota(jnp.int32, (TILE, TILE), 0)
        col = lax.broadcasted_iota(jnp.int32, (TILE, TILE), 1)
        distance = [row - col + TILE, row - col]

        def per_head(h):
            for t in range(BUCKETS):
                total = jnp.zeros((1, TILE), F32)
                for part in range(2):
                    d = distance[part]
                    inside = d >= STARTS[t]
                    if t + 1 < BUCKETS:
                        inside = inside & (d < STARTS[t + 1])
                    values = r.near[h, :, TILE * (part + 1) : TILE * (part + 2)]
                    total = total + jnp.sum(
                        jnp.where(inside, values, 0.0), axis=0, keepdims=True
                    )
                if t + 1 == BUCKETS:
                    total = total + jnp.sum(r.near[h, :, 0:TILE], axis=0, keepdims=True)
                r.sums[t : t + 1] = total
            r.g_rel[h] = lax.dot_general(
                jnp.ones((8, TILE), F32),
                r.sums[...],
                (((1,), (1,)), ((), ())),
                precision=lax.Precision.HIGHEST,
                preferred_element_type=F32,
            )

        loop(2, per_head)

    def update_tile(m):
        def step(t):
            rows = tile_of(t)
            for h in range(2):
                cols, k_cols, v_cols = head(h), head(h, base=256), head(h, base=512)
                grad = r.grad_after[m, rows, cols].astype(F32)
                u = r.update.ref[m, rows, cols]
                inverse = inverse_rms(u)
                unit = u * inverse
                forget = jax.nn.sigmoid(r.bias[:, cols] + r.slope[:, cols] * unit)
                gate = grad * (r.prior.ref[m, rows, cols].astype(F32) - unit)
                gate = gate * forget * (1.0 - forget)
                r.g_bias[:, cols] += jnp.sum(gate, axis=0, keepdims=True)
                r.g_scale[:, cols] += jnp.sum(gate * unit, axis=0, keepdims=True)
                grad_unit = grad * (1.0 - forget) + gate * r.slope[:, cols]
                inner = jnp.mean(grad_unit * unit, axis=-1, keepdims=True)
                low = (inverse * (grad_unit - unit * inner)).astype(BF)
                q = r.state_query.ref[rows, cols]
                probs = jnp.exp(nt(q, qkv[m, :, k_cols]) * scale - stats[m, rows, h : h + 1])
                grad_probs = nt(low, qkv[m, :, v_cols])
                delta = jnp.sum(probs * grad_probs, axis=-1, keepdims=True)
                grad_scores = (probs * (grad_probs - delta)).astype(BF)
                r.g_query[rows, cols] += scale * nn(grad_scores, qkv[m, :, k_cols])
                r.grad_kv[m, 512:1024, cols] += tn(grad_scores, q)
                r.grad_kv[m, 512:1024, head(h, base=256)] += tn(probs.astype(BF), low)

        return step

    def finish_rows(m):
        def step(t):
            rows = tile_of(t)
            full = r.grad_kv[m, pl.ds(pl.multiple_of(512 + t * TILE, TILE), TILE)]
            extra = r.later[m, rows].astype(F32)
            at = own_chunk(t)
            r.dqkv[m, at, :, 256:512] = (scale * full[:, 0:256] + extra[:, 0:256]).astype(BF)
            r.dqkv[m, at, :, 512:768] = (full[:, 256:512] + extra[:, 256:512]).astype(BF)

        return step

    ones = jnp.ones((8, 256), BF)

    def gain_row(part, p, rows):
        product = part * r.w.ref[p, rows].astype(F32)
        high = product.astype(BF)
        low = (product - high.astype(F32)).astype(BF)
        return (nt(ones, high) + nt(ones, low))[0:1]

    def weight_part(p, rows):
        whole, cols = r.whole.ref, slice(p * 256, (p + 1) * 256)
        part = tn(whole[0, :, :, rows].reshape(512, 256), r.dqkv[0, :, :, cols].reshape(512, 256))
        return part + tn(
            whole[1, :, :, rows].reshape(512, 256), r.dqkv[1, :, :, cols].reshape(512, 256)
        )

    def early_weights(n):
        rows = tile_of(n, 256)
        part = tn(r.att_rel.ref[0].reshape(512, 256), gm[0][:, :, rows].reshape(512, 256))
        part = part + tn(r.att_rel.ref[1].reshape(512, 256), gm[1][:, :, rows].reshape(512, 256))
        r.parts_a[rows, 256:512] = part.astype(BF)
        part = weight_part(0, rows)
        r.parts_a[rows, 0:256] = part.astype(BF)
        r.small[pl.ds(n, 1)] = gain_row(part, 0, rows)

    def end_terms(m):
        def columns(n):
            cols = tile_of(n, 256)
            part = nt(r.dqkv[m, :, :, 0:256].reshape(512, 256), r.w.ref[0, cols])
            for p in (1, 2):
                some = r.dqkv[m, :, :, p * 256 : (p + 1) * 256].reshape(512, 256)
                part = part + nt(some, r.w.ref[p, cols])
            part = part.astype(BF)
            split_rows(branch, m, cols, part)

        loop(4, columns)

    def late_weights(n):
        rows = tile_of(n, 256)
        total = r.small[pl.ds(n, 1)]
        for p in (1, 2):
            part = weight_part(p, rows)
            r.parts_b[rows, (p - 1) * 256 : p * 256] = part.astype(BF)
            total = total + gain_row(part, p, rows)
        r.small[pl.ds(n, 1)] = total / r.attn_gain[:, rows]

    def end_rows(m):
        grad_normed = ends[m].finish()
        rows = r.x.ref[m].astype(F32)
        inverse = inverse_rms(rows)
        unit = rows * inverse
        scaled = grad_normed * r.attn_gain[...]
        inner = jnp.mean(scaled * unit, axis=-1, keepdims=True)
        r.grad_x.ref[m] = r.grad_middle[m] + inverse * (scaled - unit * inner)

    def share(i):
        k, c = i // 2 + 1, i % 2
        slot = (3 - k) * 2 + core
        return remote(
            r.parts_b.at[768:784, 512:768],
            r.others.at[slot],
            r.s3.at[i],
            r.r3.at[slot],
            others[i],
        )

    def got(i):
        return remote(
            r.parts_b.at[768:784, 512:768], r.others.at[i], r.s3.at[i], r.r3.at[i], others[i]
        )

    def add_gains():
        for i in range(6):
            got(i).wait_recv()
        total = r.others[0].astype(F32)
        for i in range(1, 6):
            total = total + r.others[i].astype(F32)
        row = lax.broadcasted_iota(jnp.int32, (16, 256), 0)
        total = jnp.where(row < 8, total, 0.0) * core.astype(F32)
        at = slice(256, 272), slice(512, 768)
        r.half_b[at] = (r.half_b[at].astype(F32) + total).astype(BF)

    core_a = CoreSum(plane, r.parts_a, r.half_a)
    sum_a = PlaneReduce(plane, r.half_a, r.total_a, r.a_mid, r.a_into, r.a_quarter, r.a_small)
    all_a = PlaneGather(plane, r.total_a)
    core_b = CoreSum(plane, r.parts_b, r.half_b)
    sum_b = PlaneReduce(plane, r.half_b, r.total_b, r.b_mid, r.b_into, r.b_quarter, r.b_small)
    all_b = PlaneGather(plane, r.total_b)

    attention_rows(0)
    fourth.relay()
    for part in (r.qkv, r.kv_all, r.state_kv, r.stats, r.table):
        part.get()
    loop(4, attend(0), 1, mlp_sum.advance)
    r.prior.get()
    r.state_proj.get()
    pass_on(0)
    mlp_sum.advance()
    fourth.finish()
    attention_rows(1)
    r.branch.get()
    outs[0].start()

    def second_stage():
        mlp_sum.advance()
        mlp_all.advance()

        outs[0].relay()
        outs[1].start()

    loop(4, attend(1), 1, second_stage)
    pass_on(1)
    mlp_all.advance()
    outs[1].relay()
    r.across.get()
    r.keeps.get()
    there[0].finish()
    scan(0)
    back[0].start()
    mlp_all.advance()
    r.att_rel.get()
    r.w.get()
    r.whole.get()
    loop(4, early_weights)
    core_a.start()
    there[1].finish()
    scan(1)
    back[1].start()
    mlp_all.advance()
    bucket_sums()
    core_a.finish()
    r.middle.get()
    for m in both:
        r.out.ref[m] = r.middle.ref[m] + outs[m].finish()
    r.out.put()
    r.update.get()
    r.state_query.get()
    for m in both:
        outs[m].close()
    back[0].finish()
    loop(4, update_tile(0))
    shifts[0].wait_recv()
    loop(4, finish_rows(0))
    end_terms(0)
    ends[0].start()
    mlp_all.advance()
    back[1].finish()
    sum_a.advance()
    loop(4, update_tile(1))
    sum_a.advance()
    shifts[1].wait_recv()
    loop(4, finish_rows(1))
    ends[0].relay()
    sum_a.advance()
    loop(4, late_weights)
    for n in range(4):
        r.small[4 + n : 5 + n] = r.g_mlp_gain[:, n * 256 : (n + 1) * 256]
    r.small[8:9] = r.g_bias[...]
    r.small[9:10] = r.g_scale[...]
    r.small[10:11] = r.g_rel[0, 0:1]
    r.small[11:12] = r.g_rel[1, 0:1]
    r.small[12:16] = jnp.zeros((4, 256), F32)
    r.parts_b[0:512, 512:768] = r.g_query[...].astype(BF)
    r.parts_b[512:768, 512:768] = r.g_proj[...].reshape(256, 256).astype(BF)
    r.parts_b[768:784, 512:768] = r.small[...].astype(BF)
    r.parts_b[784:1024, 512:768] = jnp.zeros((240, 256), BF)
    core_b.start()
    for i in range(6):
        share(i).start()
    sum_a.advance()
    all_a.advance()
    end_terms(1)
    ends[1].start()
    core_b.finish()
    add_gains()
    sum_b.advance()
    all_a.advance()
    r.x.get()
    end_rows(0)
    sum_b.advance()
    ends[1].relay()
    all_a.advance()
    sum_b.advance(2)
    all_b.advance()
    all_a.advance()
    all_b.advance()
    end_rows(1)
    r.grad_x.put()
    all_b.advance()
    all_a.advance()
    all_b.advance(2)
    for step in (mlp_sum, mlp_all, core_a, sum_a, all_a, core_b, sum_b, all_b, fourth):
        step.close()
    for i in range(6):
        share(i).wait_send()
    for m in both:
        ends[m].close()
        shifts[m].wait_send()
        there[m].close()
        back[m].close()


class Late:
    def __init__(self, source, ref, sem):
        self.ref = ref
        self.copy = pltpu.make_async_copy(source, ref, sem)
        self.copy.start()
        self.open = True

    def get(self):
        if self.open:
            self.copy.wait()
            self.open = False


class Early:
    def __init__(self, target, ref, sem):
        self.ref = ref
        self.copy = pltpu.make_async_copy(ref, target, sem)
        self.sent = False

    def put(self):
        self.copy.start()
        self.sent = True


def call(kernel, name, number, now, late, small, outs, early, scratch, semaphores):
    anywhere = pl.BlockSpec(memory_space=pl.ANY)
    in_names = list(now) + list(small) + list(late)
    out_names = list(outs) + list(early)
    own = [a.shape for a in late.values()], [a.dtype for a in late.values()]
    buffers = list(zip(*own)) + list(early.values()) + list(scratch.values())

    def run(*refs):
        n, o = len(in_names), len(out_names)
        r = types.SimpleNamespace()
        held = refs[n + o : n + o + len(buffers)]
        rest = refs[n + o + len(buffers) :]
        fetch, store = rest[0], rest[1]
        for key, ref in zip(in_names[: len(now) + len(small)], refs):
            setattr(r, key, ref)
        for i, key in enumerate(late):
            setattr(r, key, Late(refs[len(now) + len(small) + i], held[i], fetch.at[i]))
        for key, ref in zip(outs, refs[n:]):
            setattr(r, key, ref)
        stores = []
        for i, key in enumerate(early):
            result = Early(refs[n + len(outs) + i], held[len(late) + i], store.at[i])
            setattr(r, key, result)
            stores.append(result)
        for key, ref in zip(scratch, held[len(late) + len(early) :]):
            setattr(r, key, ref)
        for key, ref in zip(semaphores, rest[2:]):
            setattr(r, key, ref)
        kernel(r)
        for result in stores:
            if not result.sent:
                result.put()
            result.copy.wait()

    shapes = list(outs.values()) + list(early.values())
    results = pl.pallas_call(
        run,
        out_shape=tuple(jax.ShapeDtypeStruct(shape, kind) for shape, kind in shapes),
        in_specs=[VMEM] * len(now) + [SMEM] * len(small) + [anywhere] * len(late),
        out_specs=tuple([VMEM] * len(outs) + [anywhere] * len(early)),
        scratch_shapes=[pltpu.VMEM(shape, kind) for shape, kind in buffers]
        + [sems(max(1, len(late))), sems(max(1, len(early)))]
        + list(semaphores.values()),
        compiler_params=pltpu.CompilerParams(
            collective_id=number, has_side_effects=True, vmem_limit_bytes=LIMIT
        ),
        name=name,
    )(*now.values(), *small.values(), *late.values())
    return dict(zip(out_names, results))


def finish_kernel(total_a, total_b, g_mlp, out, grad_x, state, *refs):
    results, (wide, low, some_a, some_b, rows_in, states_in, fetch, store) = refs[:14], refs[14:]
    places = [rows_in.at[0], rows_in.at[1], states_in]
    taken = [
        pltpu.make_async_copy(a, b, fetch.at[12 + i])
        for i, (a, b) in enumerate(zip((out, grad_x, state), places))
    ]
    passed = [
        pltpu.make_async_copy(a, b, store.at[i])
        for i, (a, b) in enumerate(zip(places, results[:3]))
    ]
    g_up, g_down, g_qkv, g_out, g_query, g_proj = results[3:9]
    attn_gain, mlp_gain, bias, slope, rel = results[9:]
    loads = []
    for n in range(4):
        rows = slice(n * 256, (n + 1) * 256)
        loads.append(
            [
                pltpu.make_async_copy(a.at[rows], b.at[rows], fetch.at[3 * n + i])
                for i, (a, b) in enumerate(((g_mlp, low), (total_a, some_a), (total_b, some_b)))
            ]
        )
    for copy in sum(loads, []) + taken:
        copy.start()
    stores = []

    def put(value, at, target):
        wide[at] = value.astype(F32)
        copy = pltpu.make_async_copy(wide.at[at], target, store.at[3 + len(stores)])
        copy.start()
        stores.append(copy)

    for n in range(4):
        rows = slice(n * 256, (n + 1) * 256)
        for copy in loads[n]:
            copy.wait()
        put(low[rows, 0:1024], (rows, slice(0, 1024)), g_up.at[rows])
        put(low[rows, 1024:2048], (rows, slice(1024, 2048)), g_down.at[rows])
        put(some_a[rows, 0:256], (rows, slice(2048, 2304)), g_qkv.at[0, rows])
        put(some_b[rows, 0:256], (rows, slice(2304, 2560)), g_qkv.at[1, rows])
        put(some_b[rows, 256:512], (rows, slice(2560, 2816)), g_qkv.at[2, rows])
        put(some_a[rows, 256:512], (rows, slice(2816, 3072)), g_out.at[:, rows])
    put(some_b[0:512, 512:768], (slice(0, 512), slice(3072, 3328)), g_query)
    put(some_b[512:768, 512:768], (slice(512, 768), slice(3072, 3328)), g_proj)
    for into, copy in zip(taken, passed):
        into.wait()
        copy.start()
    small = some_b[768:784, 512:768].astype(F32)
    attn_gain[...] = jnp.concatenate([small[n : n + 1] for n in range(4)], 1)
    mlp_gain[...] = jnp.concatenate([small[n : n + 1] for n in range(4, 8)], 1)
    bias[...] = small[8:9]
    slope[...] = small[9:10]
    rel[...] = small[10:12, 0:BUCKETS]
    for copy in stores + passed:
        copy.wait()


def sems(*shape):
    return pltpu.SemaphoreType.DMA(shape)


def body(
    tokens_in,
    grad_out,
    flags,
    attn_gain,
    mlp_gain,
    w_qkv,
    w_out,
    rel_bias,
    state_query,
    state_proj,
    forget_bias,
    forget_scale,
    w_up,
    w_down,
):
    micros, rows, width = tokens_in.shape
    block = rows * 4
    local = w_qkv.shape[2]
    heads = rel_bias.shape[1]
    states = state_query.shape[0]
    buckets = rel_bias.shape[0]
    count = lax.axis_size("blk")
    w = jnp.transpose(w_qkv, (1, 0, 2))
    small = dict(flags=jnp.transpose(flags))
    whole_shape = ((micros, 4, rows, width), BF)
    state_low = ((micros, states, local), BF)
    state_wide = ((micros, states, local), F32)
    rows_wide = ((micros, rows, width), F32)
    mlp_width = w_up.shape[1] + w_down.shape[1]
    exchange = dict(
        s0=sems(2),
        r0=sems(2),
        s1=sems(2, count),
        r1=sems(2, count),
        s2=sems(2, count),
        r2=sems(2, count),
        local=sems(4),
    )
    gates = dict(bias=forget_bias[None], slope=forget_scale[None])
    f = call(
        forward_kernel,
        "forward",
        1,
        dict(
            x=tokens_in,
            attn_gain=attn_gain[None],
            mlp_gain=mlp_gain[None],
            **gates,
        ),
        dict(
            w=w,
            state_query=state_query,
            g=grad_out,
            state_proj=state_proj,
            w_out=w_out,
            w_up=w_up,
            w_down=w_down,
        ),
        dict(rel=jnp.transpose(rel_bias), **small),
        dict(
            grad_middle=rows_wide,
            gm0=((4, rows, width), BF),
            half=((512, mlp_width), BF),
            g_gain=((1, width), F32),
        ),
        dict(
            whole=whole_shape,
            qkv=((micros, block, 3 * local), BF),
            kv_all=((micros, 2 * block, 2 * local), BF),
            state_kv=((micros, states, 2 * local), BF),
            prior=state_low,
            across=state_low,
            keeps=((count, 8, local), F32),
            update=state_wide,
            stats=((micros, block, TILE), F32),
            table=((heads, TILE, 5 * TILE), F32),
            state_after=state_wide,
            att_rel=((micros, 4, rows, local), BF),
            middle=rows_wide,
            branch=whole_shape,
        ),
        dict(
            whole_grad=whole_shape,
            own_keep=((8, local), F32),
            unit_low=state_low,
            held=state_low,
            terms=whole_shape,
            whole_mlp=whole_shape,
            active=((micros, block, w_up.shape[1]), BF),
            grad_hidden=((micros, block, w_up.shape[1]), BF),
            mids=((4, 4, rows // 2, width), BF),
            intos=((4, 2, rows, width), BF),
            parts=((width, mlp_width), BF),
        ),
        dict(send=sems(80), recv=sems(80), s3=sems(count), r3=sems(count), **exchange),
    )
    b = call(
        backward_kernel,
        "backward",
        2,
        dict(
            gm0=f["gm0"],
            grad_middle=f["grad_middle"],
            w_out=w_out,
            half=f["half"],
            attn_gain=attn_gain[None],
            g_mlp_gain=f["g_gain"],
            **gates,
        ),
        dict(
            qkv=f["qkv"],
            kv_all=f["kv_all"],
            state_kv=f["state_kv"],
            stats=f["stats"],
            table=f["table"],
            branch=f["branch"],
            prior=f["prior"],
            state_proj=state_proj,
            across=f["across"],
            keeps=f["keeps"],
            att_rel=f["att_rel"],
            middle=f["middle"],
            update=f["update"],
            state_query=state_query,
            w=w,
            whole=f["whole"],
            x=tokens_in,
        ),
        small,
        dict(
            total_mlp=((width, mlp_width), BF),
            total_a=((width, 512), BF),
            total_b=((width, 768), BF),
        ),
        dict(out=rows_wide, grad_x=rows_wide),
        dict(
            dqkv=((micros, 4, rows, 3 * local), BF),
            g_query=((states, local), F32),
            g_proj=(state_proj.shape, F32),
            g_rel=((heads, 8, local), F32),
            g_bias=((1, local), F32),
            g_scale=((1, local), F32),
            grad_att=((micros, block, local), BF),
            grad_kv=((micros, 2 * block, 2 * local), F32),
            grad_state=((micros, states, 2 * local), F32),
            early=((micros, block, 2 * local), BF),
            later=((micros, block, 2 * local), BF),
            grad_prior=state_low,
            moved=state_low,
            held=state_low,
            grad_after=state_low,
            near=((heads, TILE, 3 * TILE), F32),
            sums=((local, TILE), F32),
            mids=((4, 4, rows // 2, width), BF),
            intos=((4, 2, rows, width), BF),
            others=((6, 16, local), BF),
            small=((16, local), F32),
            gm1=((4, rows, width), BF),
            parts_a=((width, 512), BF),
            half_a=((512, 512), BF),
            parts_b=((width, 768), BF),
            half_b=((512, 768), BF),
            **reduce_scratch("mlp_", mlp_width),
            **reduce_scratch("a_", 512),
            **reduce_scratch("b_", 768),
        ),
        dict(send=sems(150), recv=sems(150), s3=sems(6), r3=sems(6), **exchange),
    )
    results = [
        rows_wide[0],
        rows_wide[0],
        state_wide[0],
        w_up.shape,
        w_down.shape,
        w.shape,
        w_out.shape,
        state_query.shape,
        (heads * state_proj.shape[1], local),
        (1, width),
        (1, width),
        (1, local),
        (1, local),
        (heads, buckets),
    ]
    anywhere = pl.BlockSpec(memory_space=pl.ANY)
    values = pl.pallas_call(
        finish_kernel,
        out_shape=tuple(jax.ShapeDtypeStruct(shape, F32) for shape in results),
        in_specs=[anywhere] * 6,
        out_specs=tuple([anywhere] * 9 + [VMEM] * 5),
        scratch_shapes=[
            pltpu.VMEM((width, 3328), F32),
            pltpu.VMEM((width, mlp_width), BF),
            pltpu.VMEM((width, 512), BF),
            pltpu.VMEM((width, 768), BF),
            pltpu.VMEM((2,) + rows_wide[0], F32),
            pltpu.VMEM(state_wide[0], F32),
            sems(15),
            sems(32),
        ],
        compiler_params=pltpu.CompilerParams(vmem_limit_bytes=LIMIT),
        name="finish",
    )(b["total_a"], b["total_b"], b["total_mlp"], b["out"], b["grad_x"], f["state_after"])
    out, grad_x, state_after, g_up, g_down, g_qkv, g_out, g_query, g_proj = values[:9]
    g_attn_gain, g_mlp_gain, g_bias, g_scale, g_rel = values[9:]
    return (
        out,
        grad_x,
        state_after[:, None],
        g_attn_gain[0],
        g_mlp_gain[0],
        jnp.transpose(g_qkv, (1, 0, 2)),
        g_out,
        jnp.transpose(g_rel),
        g_query,
        g_proj.reshape(state_proj.shape),
        g_bias[0],
        g_scale[0],
        g_up,
        g_down,
    )


def solution(mesh):
    return jax.shard_map(
        body,
        mesh=mesh,
        in_specs=(
            P(None, ("blk", "head"), None),
            P(None, ("blk", "head"), None),
            P(None, "blk"),
            P(),
            P(),
            P(None, None, "head"),
            P("head", None),
            P(None, "head"),
            P(None, "head"),
            P("head", None, None),
            P("head"),
            P("head"),
            P(None, "head"),
            P("head", None),
        ),
        out_specs=(
            P(None, ("blk", "head"), None),
            P(None, ("blk", "head"), None),
            P(None, "blk", None, "head"),
            P(),
            P(),
            P(None, None, "head"),
            P("head", None),
            P(None, "head"),
            P(None, "head"),
            P("head", None, None),
            P("head"),
            P("head"),
            P(None, "head"),
            P("head", None),
        ),
        check_vma=False,
    )
```

profile of v0, /device:TPU:1, one launch (start us, length us, event | category | flops | bytes accessed | tf_op | source)
XLA Modules:
  0.0 250.5 jit_solution(6190466914354611718)
XLA Ops:
  0.6 119.7 %forward.1 = (f32[2,128,1024]{2,1,0:T(8,128)}, bf16[4,128,1024]{2,1,0:T(8,128)(2,1)}, bf16[512,2048]{1,0:T(8,128)(2,1)}, f32[1,1024]{1,0:T(1,128)}, bf16[2,4,128...) custom-call(bf16[2,128,1024]{2,1,0:T(8,128)(2,1)} %refs_25_.1, ...), custom_call_target="tpu_custom_call" | custom-call | tf_op jit(solution)/shard_map/forward/pallas_call | solution.py:1233
  120.3 120.6 %backward.1 = (bf16[1024,2048]{1,0:T(8,128)(2,1)}, bf16[1024,512]{1,0:T(8,128)(2,1)}, bf16[1024,768]{1,0:T(8,128)(2,1)}, f32[2,128,1024]{2,1,0:T(8,128)}, f32[2,128,1024]{2,1,0:T(8,128)}) custom-call(bf16[4,128,1024]{2,1,0:T(8,128)(2,1)} %get-tuple-element.51.refs_0_, f32[2,128,1024]{2,1,0:T(8,128)} %get-tuple-element.52.refs_1_, bf16[256,1024]{1,0:T(8,128)(2,1)} %refs_2_.1, ...), custom_call_target="tpu_custom_call" | custom-call | tf_op jit(solution)/shard_map/backward/pallas_call | solution.py:1233
  241.0 9.4 %finish.1 = (f32[2,128,1024]{2,1,0:T(8,128)}, f32[2,128,1024]{2,1,0:T(8,128)}, f32[2,512,256]{2,1,0:T(8,128)}, f32[1024,1024]{1,0:T(8,128)}, f32[1024,1024]{1,0:...) custom-call(bf16[1024,512]{1,0:T(8,128)(2,1)} %get-tuple-element.68., ...), custom_call_target="tpu_custom_call" | custom-call | tf_op jit(solution)/shard_map/finish/pallas_call | solution.py:1496
where the time goes:
time: 251 us
  Pallas kernels  250 us (100%)
    pallas_call x2, Pallas kernels, call(): pl.pallas_call(run, out_shape=tuple((jax.ShapeDtypeStruct(shape, kind) fo...  240 us
    pallas_call x1, Pallas kernels, body(): pl.pallas_call(finish_kernel, out_shape=tuple((jax.ShapeDtypeStruct(shape...  9.35 us

commit v1 on v0

--- a/solution.py
+++ b/solution.py
@@ -680,7 +680,7 @@
         total = total + tn(r.active[1, :, rows], r.whole_grad[1].reshape(512, 1024))
         r.parts[rows, 1024:2048] = total.astype(BF)
 
-    cores = CoreSum(plane, r.parts, r.half)
+    cores = CoreSum(plane, r.parts, r.half.ref)
 
     gather_x[0].relay()
     gather_x[1].start()
@@ -766,6 +766,7 @@
     branch_terms(1)
     r.branch.put()
     cores.finish()
+    r.half.put()
     grad_rows(1)
     fourth.finish()
     cores.close()
@@ -799,10 +800,9 @@
     fourth = Gather(ring, by_rows(r.gm1))
     fourth.start()
     mlp_sum = PlaneReduce(
-        plane, r.half, r.total_mlp, r.mlp_mid, r.mlp_into, r.mlp_quarter, r.mlp_small
+        plane, r.half.ref, r.total_mlp.ref, r.mlp_mid, r.mlp_into, r.mlp_quarter, r.mlp_small
     )
-    mlp_all = PlaneGather(plane, r.total_mlp)
-    mlp_sum.advance()
+    mlp_all = PlaneGather(plane, r.total_mlp.ref)
     qkv, kv_all, state_kv, stats = r.qkv.ref, r.kv_all.ref, r.state_kv.ref, r.stats.ref
     r.branch.get()
     branch = r.branch.ref
@@ -1060,9 +1060,10 @@
 
     attention_rows(0)
     fourth.relay()
-    for part in (r.qkv, r.kv_all, r.state_kv, r.stats, r.table):
+    for part in (r.half, r.qkv, r.kv_all, r.state_kv, r.stats, r.table):
         part.get()
-    loop(4, attend(0), 1, mlp_sum.advance)
+    mlp_sum.advance()
+    loop(4, attend(0))
     r.prior.get()
     r.state_proj.get()
     pass_on(0)
@@ -1072,23 +1073,20 @@
     r.branch.get()
     outs[0].start()
 
-    def second_stage():
+    def between():
         mlp_sum.advance()
-        mlp_all.advance()
-
         outs[0].relay()
         outs[1].start()
 
-    loop(4, attend(1), 1, second_stage)
+    loop(4, attend(1), 1, between)
     pass_on(1)
-    mlp_all.advance()
     outs[1].relay()
     r.across.get()
     r.keeps.get()
     there[0].finish()
     scan(0)
     back[0].start()
-    mlp_all.advance()
+    mlp_sum.advance()
     r.att_rel.get()
     r.w.get()
     r.whole.get()
@@ -1097,7 +1095,6 @@
     there[1].finish()
     scan(1)
     back[1].start()
-    mlp_all.advance()
     bucket_sums()
     core_a.finish()
     r.middle.get()
@@ -1109,20 +1106,19 @@
     for m in both:
         outs[m].close()
     back[0].finish()
+    mlp_all.advance()
     loop(4, update_tile(0))
     shifts[0].wait_recv()
     loop(4, finish_rows(0))
     end_terms(0)
     ends[0].start()
+    back[1].finish()
     mlp_all.advance()
-    back[1].finish()
-    sum_a.advance()
     loop(4, update_tile(1))
-    sum_a.advance()
     shifts[1].wait_recv()
     loop(4, finish_rows(1))
     ends[0].relay()
-    sum_a.advance()
+    mlp_all.advance()
     loop(4, late_weights)
     for n in range(4):
         r.small[4 + n : 5 + n] = r.g_mlp_gain[:, n * 256 : (n + 1) * 256]
@@ -1139,27 +1135,35 @@
     for i in range(6):
         share(i).start()
     sum_a.advance()
-    all_a.advance()
+    mlp_all.advance()
     end_terms(1)
     ends[1].start()
     core_b.finish()
     add_gains()
     sum_b.advance()
-    all_a.advance()
+    sum_a.advance()
     r.x.get()
     end_rows(0)
     sum_b.advance()
     ends[1].relay()
+    mlp_all.advance()
+    r.total_mlp.put()
+    sum_a.advance()
+    sum_b.advance()
+    sum_a.advance()
     all_a.advance()
-    sum_b.advance(2)
+    sum_b.advance()
     all_b.advance()
     all_a.advance()
     all_b.advance()
     end_rows(1)
     r.grad_x.put()
+    all_a.advance()
     all_b.advance()
     all_a.advance()
-    all_b.advance(2)
+    all_b.advance()
+    all_a.advance()
+    all_b.advance()
     for step in (mlp_sum, mlp_all, core_a, sum_a, all_a, core_b, sum_b, all_b, fourth):
         step.close()
     for i in range(6):
@@ -1370,7 +1374,6 @@
         dict(
             grad_middle=rows_wide,
             gm0=((4, rows, width), BF),
-            half=((512, mlp_width), BF),
             g_gain=((1, width), F32),
         ),
         dict(
@@ -1388,6 +1391,7 @@
             att_rel=((micros, 4, rows, local), BF),
             middle=rows_wide,
             branch=whole_shape,
+            half=((512, mlp_width), BF),
         ),
         dict(
             whole_grad=whole_shape,
@@ -1412,12 +1416,12 @@
             gm0=f["gm0"],
             grad_middle=f["grad_middle"],
             w_out=w_out,
-            half=f["half"],
             attn_gain=attn_gain[None],
             g_mlp_gain=f["g_gain"],
             **gates,
         ),
         dict(
+            half=f["half"],
             qkv=f["qkv"],
             kv_all=f["kv_all"],
             state_kv=f["state_kv"],
@@ -1438,11 +1442,10 @@
         ),
         small,
         dict(
-            total_mlp=((width, mlp_width), BF),
             total_a=((width, 512), BF),
             total_b=((width, 768), BF),
         ),
-        dict(out=rows_wide, grad_x=rows_wide),
+        dict(out=rows_wide, grad_x=rows_wide, total_mlp=((width, mlp_width), BF)),
         dict(
             dqkv=((micros, 4, rows, 3 * local), BF),
             g_query=((states, local), F32),

time: 251 us -> 239 us (0.952)
  Pallas kernels: 250 us -> 238 us
    pallas_call x2, Pallas kernels: 240 us -> 228 us  [call(): pl.pallas_call(run, out_shape=tuple((jax.ShapeDtypeStruct(shape, kind) fo...]
where the time goes in v1:
time: 239 us
  Pallas kernels  238 us (100%)
    pallas_call x2, Pallas kernels, call(): pl.pallas_call(run, out_shape=tuple((jax.ShapeDtypeStruct(shape, kind) fo...  228 us
    pallas_call x1, Pallas kernels, body(): pl.pallas_call(finish_kernel, out_shape=tuple((jax.ShapeDtypeStruct(shape...  9.35 us

profile of v1, /device:TPU:1, one launch (start us, length us, event | category | flops | bytes accessed | tf_op | source)
XLA Modules:
  0.0 238.6 jit_solution(13115651456865561395)
XLA Ops:
  0.6 118.8 %forward.1 = (f32[2,128,1024]{2,1,0:T(8,128)}, bf16[4,128,1024]{2,1,0:T(8,128)(2,1)}, f32[1,1024]{1,0:T(1,128)}, bf16[2,4,128,1024]{3,2,1,0:T(8,128)(2,1)}, bf16...) custom-call(bf16[2,128,1024]{2,1,0:T(8,128)(2,1)} %refs_25_.1, ...), custom_call_target="tpu_custom_call" | custom-call | tf_op jit(solution)/shard_map/forward/pallas_call | solution.py:1237
  119.5 109.6 %backward.1 = (bf16[1024,512]{1,0:T(8,128)(2,1)}, bf16[1024,768]{1,0:T(8,128)(2,1)}, f32[2,128,1024]{2,1,0:T(8,128)}, f32[2,128,1024]{2,1,0:T(8,128)}, bf16[1024,2048]{1,0:T(8,128)(2,1)}) custom-call(bf16[4,128,1024]{2,1,0:T(8,128)(2,1)} %get-tuple-element.51.refs_0_, f32[2,128,1024]{2,1,0:T(8,128)} %get-tuple-element.52.refs_1_, bf16[256,1024]{1,0:T(8,128)(2,1)} %refs_2_.1, ...), custom_call_target="tpu_custom_call" | custom-call | tf_op jit(solution)/shard_map/backward/pallas_call | solution.py:1237
  229.1 9.4 %finish.1 = (f32[2,128,1024]{2,1,0:T(8,128)}, f32[2,128,1024]{2,1,0:T(8,128)}, f32[2,512,256]{2,1,0:T(8,128)}, f32[1024,1024]{1,0:T(8,128)}, f32[1024,1024]{1,0:...) custom-call(bf16[1024,512]{1,0:T(8,128)(2,1)} %get-tuple-element.68., ...), custom_call_target="tpu_custom_call" | custom-call | tf_op jit(solution)/shard_map/finish/pallas_call | solution.py:1499

commit v2 on v1

--- a/solution.py
+++ b/solution.py
@@ -404,9 +404,19 @@
         return remote(
             self.source.at[tile_of(peer, self.size)],
             self.target.at[tile_of(self.place, self.size)],
-            self.send.at[j],
-            self.recv.at[j],
+            self.send,
+            self.recv,
             {"blk": peer},
+        )
+
+    def all(self):
+        rows = slice(0, (self.count - 1) * self.size)
+        return remote(
+            self.source.at[rows],
+            self.target.at[rows],
+            self.send,
+            self.recv,
+            {"blk": lax.rem(self.place + 1, self.count)},
         )
 
     def own(self):
@@ -419,10 +429,10 @@
 
     def finish(self):
         self.own().wait()
-        loop(self.count - 1, lambda j: self.part(j + 1).wait_recv())
+        self.all().wait_recv()
 
     def close(self):
-        loop(self.count - 1, lambda j: self.part(j + 1).wait_send())
+        self.all().wait_send()
 
 
 def greet_blocks():
@@ -487,12 +497,13 @@
         rows = r.x[m].astype(F32)
         r.whole.ref[m, 0] = (rows * inverse_rms(rows) * r.attn_gain[...]).astype(BF)
 
+    greeted = ring.greet() + greet_blocks()
     norm_rows(0)
     for m in both:
         keep = 1.0 - r.flags[0, m].astype(F32)
-        r.own_keep[m : m + 1] = jnp.full((1, 256), keep, F32)
-    r.own_keep[2:8] = jnp.zeros((6, 256), F32)
-    pl.semaphore_wait(pltpu.get_barrier_semaphore(), ring.greet() + greet_blocks())
+        r.own_keep[0, m : m + 1] = jnp.full((1, 256), keep, F32)
+    r.own_keep[0, 2:8] = jnp.zeros((6, 256), F32)
+    pl.semaphore_wait(pltpu.get_barrier_semaphore(), greeted)
     whole, qkv, kv_all = r.whole.ref, r.qkv.ref, r.kv_all.ref
     prior, across, keeps = r.prior.ref, r.across.ref, r.keeps.ref
     update, stats, state_kv = r.update.ref, r.stats.ref, r.state_kv.ref
@@ -504,10 +515,15 @@
 
     def tell(j):
         peer = {"blk": lax.rem(place + j, count)}
-        return remote(r.own_keep, keeps.at[place], r.s3.at[j], r.r3.at[j], peer)
+        return remote(r.own_keep.at[0], keeps.at[place], r.s3.at[0], r.r3.at[0], peer)
+
+    def tell_all():
+        peer = {"blk": lax.rem(place + 1, count)}
+        rows = slice(0, count - 1)
+        return remote(r.own_keep.at[rows], keeps.at[rows], r.s3.at[0], r.r3.at[0], peer)
 
     loop(count - 1, lambda j: tell(j + 1).start())
-    keeps[place] = r.own_keep[...]
+    keeps[place] = r.own_keep[0]
     write_table(table, r.rel)
     r.table.put()
     after = {"blk": lax.rem(place + 1, count)}
@@ -704,7 +720,7 @@
     r.update.put()
     gather_g[0].relay()
     gather_g[1].start()
-    loop(count - 1, lambda j: tell(j + 1).wait_recv())
+    tell_all().wait_recv()
     there[0].finish()
     scan(0)
     back[0].start()
@@ -777,7 +793,7 @@
         shifts[m].wait_send()
         there[m].close()
         back[m].close()
-    loop(count - 1, lambda j: tell(j + 1).wait_send())
+    tell_all().wait_send()
 
 
 def backward_kernel(r):
@@ -788,7 +804,6 @@
     place, count = lax.axis_index("blk"), lax.axis_size("blk")
     both = range(2)
     gm = [r.gm0, r.gm1]
-    r.gm1[0] = r.grad_middle[1].astype(BF)
     core = place % 2
     others = [
         {"head": ring.chunk(k), "blk": place - core + c} for k in range(1, 4) for c in range(2)
@@ -796,7 +811,9 @@
     barrier = pltpu.get_barrier_semaphore()
     for device in others:
         pl.semaphore_signal(barrier, inc=1, device_id=device, device_id_type=MESH)
-    pl.semaphore_wait(barrier, len(others) + greet_blocks())
+    greeted = len(others) + greet_blocks()
+    r.gm1[0] = r.grad_middle[1].astype(BF)
+    pl.semaphore_wait(barrier, greeted)
     fourth = Gather(ring, by_rows(r.gm1))
     fourth.start()
     mlp_sum = PlaneReduce(
@@ -1344,10 +1361,10 @@
     exchange = dict(
         s0=sems(2),
         r0=sems(2),
-        s1=sems(2, count),
-        r1=sems(2, count),
-        s2=sems(2, count),
-        r2=sems(2, count),
+        s1=sems(2),
+        r1=sems(2),
+        s2=sems(2),
+        r2=sems(2),
         local=sems(4),
     )
     gates = dict(bias=forget_bias[None], slope=forget_scale[None])
@@ -1395,7 +1412,7 @@
         ),
         dict(
             whole_grad=whole_shape,
-            own_keep=((8, local), F32),
+            own_keep=((count, 8, local), F32),
             unit_low=state_low,
             held=state_low,
             terms=whole_shape,
@@ -1406,7 +1423,7 @@
             intos=((4, 2, rows, width), BF),
             parts=((width, mlp_width), BF),
         ),
-        dict(send=sems(80), recv=sems(80), s3=sems(count), r3=sems(count), **exchange),
+        dict(send=sems(80), recv=sems(80), s3=sems(1), r3=sems(1), **exchange),
     )
     b = call(
         backward_kernel,

time: 239 us -> 232 us (0.971)
  Pallas kernels: 238 us -> 231 us
    pallas_call x2, Pallas kernels: 228 us -> 222 us  [call(): pl.pallas_call(run, out_shape=tuple((jax.ShapeDtypeStruct(shape, kind) fo...]
where the time goes in v2:
time: 232 us
  Pallas kernels  231 us (100%)
    pallas_call x2, Pallas kernels, call(): pl.pallas_call(run, out_shape=tuple((jax.ShapeDtypeStruct(shape, kind) fo...  222 us
    pallas_call x1, Pallas kernels, body(): pl.pallas_call(finish_kernel, out_shape=tuple((jax.ShapeDtypeStruct(shape...  9.35 us

profile of v2, /device:TPU:1, one launch (start us, length us, event | category | flops | bytes accessed | tf_op | source)
XLA Modules:
  0.0 231.8 jit_solution(3307361522770344170)
XLA Ops:
  0.6 115.0 %forward.1 = (f32[2,128,1024]{2,1,0:T(8,128)}, bf16[4,128,1024]{2,1,0:T(8,128)(2,1)}, f32[1,1024]{1,0:T(1,128)}, bf16[2,4,128,1024]{3,2,1,0:T(8,128)(2,1)}, bf16...) custom-call(bf16[2,128,1024]{2,1,0:T(8,128)(2,1)} %refs_25_.1, ...), custom_call_target="tpu_custom_call" | custom-call | tf_op jit(solution)/shard_map/forward/pallas_call | solution.py:1254
  115.7 106.6 %backward.1 = (bf16[1024,512]{1,0:T(8,128)(2,1)}, bf16[1024,768]{1,0:T(8,128)(2,1)}, f32[2,128,1024]{2,1,0:T(8,128)}, f32[2,128,1024]{2,1,0:T(8,128)}, bf16[1024,2048]{1,0:T(8,128)(2,1)}) custom-call(bf16[4,128,1024]{2,1,0:T(8,128)(2,1)} %get-tuple-element.51.refs_0_, f32[2,128,1024]{2,1,0:T(8,128)} %get-tuple-element.52.refs_1_, bf16[256,1024]{1,0:T(8,128)(2,1)} %refs_2_.1, ...), custom_call_target="tpu_custom_call" | custom-call | tf_op jit(solution)/shard_map/backward/pallas_call | solution.py:1254
  222.3 9.4 %finish.1 = (f32[2,128,1024]{2,1,0:T(8,128)}, f32[2,128,1024]{2,1,0:T(8,128)}, f32[2,512,256]{2,1,0:T(8,128)}, f32[1024,1024]{1,0:T(8,128)}, f32[1024,1024]{1,0:...) custom-call(bf16[1024,512]{1,0:T(8,128)(2,1)} %get-tuple-element.68., ...), custom_call_target="tpu_custom_call" | custom-call | tf_op jit(solution)/shard_map/finish/pallas_call | solution.py:1516

commit v3 on v2

--- a/solution.py
+++ b/solution.py
@@ -567,15 +567,18 @@
         return step
 
     def scan(m):
-        def step(b, state):
-            rows = tile_of(b, 16)
-            u = across[m, rows].astype(F32)
-            forget = jax.nn.sigmoid(r.bias[...] + r.slope[...] * u)
-            before = keeps[b, m : m + 1] * state
-            r.held[m, rows] = before.astype(BF)
-            return forget * before + (1.0 - forget) * u
-
-        lax.fori_loop(0, count, step, jnp.zeros((16, 256), F32))
+        def step(g, state):
+            for k in range(4):
+                b = g * 4 + k
+                rows = tile_of(b, 16)
+                u = across[m, rows].astype(F32)
+                forget = jax.nn.sigmoid(r.bias[...] + r.slope[...] * u)
+                before = keeps[b, m : m + 1] * state
+                r.held[m, rows] = before.astype(BF)
+                state = forget * before + (1.0 - forget) * u
+            return state
+
+        lax.fori_loop(0, count // 4, step, jnp.zeros((16, 256), F32))
 
     def state(m):
         def step(t):
@@ -813,6 +816,8 @@
         pl.semaphore_signal(barrier, inc=1, device_id=device, device_id_type=MESH)
     greeted = len(others) + greet_blocks()
     r.gm1[0] = r.grad_middle[1].astype(BF)
+    for ref in (r.near, r.sums, r.g_query, r.g_bias, r.g_scale, r.grad_kv, r.grad_state):
+        ref[...] = jnp.zeros(ref.shape, F32)
     pl.semaphore_wait(barrier, greeted)
     fourth = Gather(ring, by_rows(r.gm1))
     fourth.start()
@@ -839,8 +844,6 @@
         Exchange(r.held.at[m], r.grad_after.at[m], r.s2.at[m], r.r2.at[m], r.local.at[2 + m])
         for m in both
     ]
-    for ref in (r.near, r.sums, r.g_query, r.g_bias, r.g_scale, r.grad_kv, r.grad_state):
-        ref[...] = jnp.zeros(ref.shape, F32)
 
     def own_chunk(qi):
         return lax.rem(qi + 4 - ring.me, 4)
@@ -867,8 +870,9 @@
                 from_state = jnp.exp(nt(q, state_kv[m, :, sk_cols]) * scale - level)
                 grad_token = nt(d, kv_all[m, window, v_cols])
                 grad_from = nt(d, state_kv[m, :, sv_cols])
-                delta = jnp.sum(token * grad_token, axis=-1, keepdims=True) + jnp.sum(
-                    from_state * grad_from, axis=-1, keepdims=True
+                attended = r.att_rel.ref[m, own_chunk(qi), :, head(h)]
+                delta = jnp.sum(
+                    d.astype(F32) * attended.astype(F32), axis=-1, keepdims=True
                 )
                 grad_token = token * (grad_token - delta)
                 grad_from = from_state * (grad_from - delta)
@@ -907,16 +911,18 @@
         shifts[m].start()
 
     def scan(m):
-        def step(t, grad):
-            b = count - 1 - t
-            rows = tile_of(b, 16)
-            r.held[m, rows] = grad.astype(BF)
-            u = r.across.ref[m, rows].astype(F32)
-            forget = jax.nn.sigmoid(r.bias[...] + r.slope[...] * u)
-            moved = r.moved[m, rows].astype(F32)
-            return r.keeps.ref[b, m : m + 1] * (moved + forget * grad)
-
-        lax.fori_loop(0, count, step, jnp.zeros((16, 256), F32))
+        def step(g, grad):
+            for k in range(4):
+                b = count - 1 - (g * 4 + k)
+                rows = tile_of(b, 16)
+                r.held[m, rows] = grad.astype(BF)
+                u = r.across.ref[m, rows].astype(F32)
+                forget = jax.nn.sigmoid(r.bias[...] + r.slope[...] * u)
+                moved = r.moved[m, rows].astype(F32)
+                grad = r.keeps.ref[b, m : m + 1] * (moved + forget * grad)
+            return grad
+
+        lax.fori_loop(0, count // 4, step, jnp.zeros((16, 256), F32))
 
     def bucket_sums():
         row = lax.broadcasted_iota(jnp.int32, (TILE, TILE), 0)
@@ -1077,7 +1083,7 @@
 
     attention_rows(0)
     fourth.relay()
-    for part in (r.half, r.qkv, r.kv_all, r.state_kv, r.stats, r.table):
+    for part in (r.half, r.qkv, r.kv_all, r.state_kv, r.stats, r.table, r.att_rel):
         part.get()
     mlp_sum.advance()
     loop(4, attend(0))
@@ -1439,6 +1445,7 @@
         ),
         dict(
             half=f["half"],
+            att_rel=f["att_rel"],
             qkv=f["qkv"],
             kv_all=f["kv_all"],
             state_kv=f["state_kv"],
@@ -1449,7 +1456,6 @@
             state_proj=state_proj,
             across=f["across"],
             keeps=f["keeps"],
-            att_rel=f["att_rel"],
             middle=f["middle"],
             update=f["update"],
             state_query=state_query,

time: 232 us -> 232 us (level)
  no operation moved by 1% of the time
where the time goes in v3:
time: 232 us
  Pallas kernels  231 us (100%)
    pallas_call x2, Pallas kernels, call(): pl.pallas_call(run, out_shape=tuple((jax.ShapeDtypeStruct(shape, kind) fo...  221 us
    pallas_call x1, Pallas kernels, body(): pl.pallas_call(finish_kernel, out_shape=tuple((jax.ShapeDtypeStruct(shape...  9.35 us

profile of v3, /device:TPU:1, one launch (start us, length us, event | category | flops | bytes accessed | tf_op | source)
XLA Modules:
  0.0 231.6 jit_solution(16216593642494528572)
XLA Ops:
  0.6 115.1 %forward.1 = (f32[2,128,1024]{2,1,0:T(8,128)}, bf16[4,128,1024]{2,1,0:T(8,128)(2,1)}, f32[1,1024]{1,0:T(1,128)}, bf16[2,4,128,1024]{3,2,1,0:T(8,128)(2,1)}, bf16...) custom-call(bf16[2,128,1024]{2,1,0:T(8,128)(2,1)} %refs_25_.1, ...), custom_call_target="tpu_custom_call" | custom-call | tf_op jit(solution)/shard_map/forward/pallas_call | solution.py:1260
  115.8 106.2 %backward.1 = (bf16[1024,512]{1,0:T(8,128)(2,1)}, bf16[1024,768]{1,0:T(8,128)(2,1)}, f32[2,128,1024]{2,1,0:T(8,128)}, f32[2,128,1024]{2,1,0:T(8,128)}, bf16[1024,2048]{1,0:T(8,128)(2,1)}) custom-call(bf16[4,128,1024]{2,1,0:T(8,128)(2,1)} %get-tuple-element.51.refs_0_, f32[2,128,1024]{2,1,0:T(8,128)} %get-tuple-element.52.refs_1_, bf16[256,1024]{1,0:T(8,128)(2,1)} %refs_2_.1, ...), custom_call_target="tpu_custom_call" | custom-call | tf_op jit(solution)/shard_map/backward/pallas_call | solution.py:1260
  222.1 9.4 %finish.1 = (f32[2,128,1024]{2,1,0:T(8,128)}, f32[2,128,1024]{2,1,0:T(8,128)}, f32[2,512,256]{2,1,0:T(8,128)}, f32[1024,1024]{1,0:T(8,128)}, f32[1024,1024]{1,0:...) custom-call(bf16[1024,512]{1,0:T(8,128)(2,1)} %get-tuple-element.68., ...), custom_call_target="tpu_custom_call" | custom-call | tf_op jit(solution)/shard_map/finish/pallas_call | solution.py:1522
